TPU v7x, 32 devices: a whole 2x2x4 slice. The times are simulated.
32 devices in a mesh: rows: 8 (over z, x), blk: 4 (over y, core).
Axes of the slice: x: 2, y: 2, z: 4, core: 2. Of those that a mesh axis runs over, the one named last changes fastest.
Arguments:
- tokens: bfloat16 [32, 1024, 512], P('rows', 'blk'), may hold values from -6 to 6
- seg_lengths: int32 [32, 8], P('rows'), may hold values from 1 to 1017, as said below
- ln1_gain: float32 [512], replicated, may hold values from 0.25 to 1.75
- ln1_bias: float32 [512], replicated, may hold values from -1 to 1
- w_qkv: bfloat16 [512, 1536], replicated, may hold values from -0.25 to 0.25
- b_qv: float32 [1024], replicated, may hold values from -1 to 1
- w_o: bfloat16 [512, 512], replicated, may hold values from -1 to 1
- b_o: float32 [512], replicated, may hold values from -1 to 1
- ln2_gain: float32 [512], replicated, may hold values from 0.25 to 1.75
- ln2_bias: float32 [512], replicated, may hold values from -1 to 1
- w_up: bfloat16 [512, 1024], replicated, may hold values from -0.25 to 0.25
- b_up: float32 [1024], replicated, may hold values from -1 to 1
- w_down: bfloat16 [1024, 512], replicated, may hold values from -0.1875 to 0.1875
- b_down: float32 [512], replicated, may hold values from -1 to 1
- cotangent: bfloat16 [32, 1024, 512], P('rows', 'blk'), may hold values from -6 to 6
Outputs:
- output: bfloat16 [32, 1024, 512], P('rows', 'blk')
- input_grad: float32 [32, 1024, 512], P('rows', 'blk')
- grad_ln1_gain: float32 [512], replicated
- grad_ln1_bias: float32 [512], replicated
- grad_w_qkv: float32 [512, 1536], replicated
- grad_b_qv: float32 [1024], replicated
- grad_w_o: float32 [512, 512], replicated
- grad_b_o: float32 [512], replicated
- grad_ln2_gain: float32 [512], replicated
- grad_ln2_bias: float32 [512], replicated
- grad_w_up: float32 [512, 1024], replicated
- grad_b_up: float32 [1024], replicated
- grad_w_down: float32 [1024, 512], replicated
- grad_b_down: float32 [512], replicated
Inputs may be any that keep to these rules, and one draw needn't show every extreme that they name: `seg_lengths`: each row's 8 cell lengths sum to 1024; in each aligned block of 4 rows that starts at a multiple of 4, one row holds a cell of exactly 1017 tokens.
All inputs are finite; a program needn't handle non-finite values.
Results may differ from a plain program's by a relative error of at most 0.009.
Values may be sent and summed in bfloat16 or wider, within the bound.
No kernel may reach another device: no remote copies, remote signals or barrier semaphores. Data moves between devices by JAX's collectives and lax.ppermute only.
A program may use at most 192 MiB of HBM per device.

v0:
```python
import jax
import jax.numpy as jnp
from jax import lax
from jax.sharding import PartitionSpec as P

HEADS = 8


norm_eps = 1e-05
neg_big = -1e30


def layer_norm(values, gain_vec, bias_vec):
    average = jnp.mean(values, axis=-1, keepdims=True)
    centered = values - average
    variance = jnp.mean(centered * centered, axis=-1, keepdims=True)
    return centered * lax.rsqrt(variance + norm_eps) * gain_vec + bias_vec


def segment_of(cell_ends, positions):
    return jnp.sum((cell_ends[:, None, :] <= positions[None, :, None]).astype(jnp.int32), axis=-1)


def block_scores(query_heads, key_heads, query_pos, key_pos, query_seg, key_seg, scale_qk):
    raw_scores = (
        jnp.einsum("rqhd,rkhd->rqhk", query_heads, key_heads, preferred_element_type=jnp.float32)
        * scale_qk
    )
    causal = key_pos[None, :] <= query_pos[:, None]
    same_cell = query_seg[:, :, None] == key_seg[:, None, :]
    allowed = (causal[None] & same_cell)[:, :, None, :]
    return (jnp.where(allowed, raw_scores, neg_big), allowed)


def block_active(query_pos, key_pos, query_seg, key_seg):
    return (key_pos[0] <= query_pos[-1]) & jnp.any(key_seg[:, -1] >= query_seg[:, 0])


def backward_block(
    query_heads,
    grad_heads,
    log_total,
    delta_sum,
    key_heads,
    value_heads,
    query_pos,
    key_pos,
    query_seg,
    key_seg,
    scale_qk,
):
    scores, allowed = block_scores(
        query_heads, key_heads, query_pos, key_pos, query_seg, key_seg, scale_qk
    )
    softmaxed = jnp.where(allowed, jnp.exp(scores - log_total[..., None]), 0.0)
    grad_probs = jnp.einsum(
        "rqhd,rkhd->rqhk", grad_heads, value_heads, preferred_element_type=jnp.float32
    )
    grad_scores = (softmaxed * (grad_probs - delta_sum[..., None])).astype(jnp.bfloat16)
    grad_query = (
        jnp.einsum("rqhk,rkhd->rqhd", grad_scores, key_heads, preferred_element_type=jnp.float32)
        * scale_qk
    )
    grad_key = (
        jnp.einsum("rqhk,rqhd->rkhd", grad_scores, query_heads, preferred_element_type=jnp.float32)
        * scale_qk
    )
    grad_value = jnp.einsum(
        "rqhk,rqhd->rkhd",
        softmaxed.astype(jnp.bfloat16),
        grad_heads,
        preferred_element_type=jnp.float32,
    )
    return (grad_query, grad_key, grad_value)


def unchanged(old_state):
    return old_state


def per_device(
    tokens,
    seg_lengths,
    ln1_gain,
    ln1_bias,
    w_qkv,
    b_qv,
    w_o,
    b_o,
    ln2_gain,
    ln2_bias,
    w_up,
    b_up,
    w_down,
    b_down,
    cotangent,
):
    row_count, slice_len, width_all = tokens.shape
    head_size = width_all // HEADS
    scale_qk = head_size ** (-0.5)
    head_shape = (row_count, slice_len, HEADS, head_size)
    stat_shape = (row_count, slice_len, HEADS)
    full_length = lax.axis_size("blk") * slice_len
    offsets = jnp.arange(slice_len, dtype=jnp.int32)
    query_pos = lax.axis_index("blk") * slice_len + offsets
    cell_ends = jnp.cumsum(seg_lengths, axis=1)
    query_seg = segment_of(cell_ends, query_pos)

    def take_block(piece, block_index):
        return lax.dynamic_slice_in_dim(piece, block_index * slice_len, slice_len, 1).reshape(
            head_shape
        )

    inputs = tokens.astype(jnp.float32)
    normed_val, first_pull = jax.vjp(layer_norm, inputs, ln1_gain, ln1_bias)
    normed_one = normed_val.astype(jnp.bfloat16)
    projected = jnp.dot(normed_one, w_qkv, preferred_element_type=jnp.float32)
    query_b = (projected[..., :width_all] + b_qv[:width_all]).astype(jnp.bfloat16)
    key_b = projected[..., width_all : 2 * width_all].astype(jnp.bfloat16)
    value_b = (projected[..., 2 * width_all :] + b_qv[width_all:]).astype(jnp.bfloat16)
    query_heads = query_b.reshape(head_shape)
    start_state = (
        jnp.full(stat_shape, neg_big, jnp.float32),
        jnp.zeros(stat_shape, jnp.float32),
        jnp.zeros(head_shape, jnp.float32),
    )
    key_piece = lax.all_gather(key_b, "blk", axis=1, tiled=True)
    value_piece = lax.all_gather(value_b, "blk", axis=1, tiled=True)

    def forward_block_step(block_index, inner_state):
        key_pos = block_index * slice_len + offsets
        key_seg = segment_of(cell_ends, key_pos)
        key_heads = take_block(key_piece, block_index)
        value_heads = take_block(value_piece, block_index)

        def forward_update(old_state):
            running_top, running_total, running_sum = old_state
            scores, allowed = block_scores(
                query_heads, key_heads, query_pos, key_pos, query_seg, key_seg, scale_qk
            )
            new_top = jnp.maximum(running_top, jnp.max(scores, axis=-1))
            factor = jnp.exp(running_top - new_top)
            weights_now = jnp.where(allowed, jnp.exp(scores - new_top[..., None]), 0.0)
            new_total = running_total * factor + jnp.sum(weights_now, axis=-1)
            new_sum = running_sum * factor[..., None] + jnp.einsum(
                "rqhk,rkhd->rqhd",
                weights_now.astype(jnp.bfloat16),
                value_heads,
                preferred_element_type=jnp.float32,
            )
            return (new_top, new_total, new_sum)

        return lax.cond(
            block_active(query_pos, key_pos, query_seg, key_seg),
            forward_update,
            unchanged,
            inner_state,
        )

    running_top, running_total, running_sum = lax.fori_loop(
        0, key_piece.shape[1] // slice_len, forward_block_step, start_state
    )
    attn_f32 = (running_sum / running_total[..., None]).reshape(row_count, slice_len, width_all)
    log_total = running_top + jnp.log(running_total)
    attn_b = attn_f32.astype(jnp.bfloat16)
    middle = inputs + jnp.dot(attn_b, w_o, preferred_element_type=jnp.float32) + b_o
    normed_two_val, second_pull = jax.vjp(layer_norm, middle, ln2_gain, ln2_bias)
    normed_two = normed_two_val.astype(jnp.bfloat16)
    hidden_pre = jnp.dot(normed_two, w_up, preferred_element_type=jnp.float32) + b_up
    hidden_val, gelu_pull = jax.vjp(jax.nn.gelu, hidden_pre)
    hidden_b = hidden_val.astype(jnp.bfloat16)
    output = (
        middle + jnp.dot(hidden_b, w_down, preferred_element_type=jnp.float32) + b_down
    ).astype(jnp.bfloat16)
    grad_out = cotangent.astype(jnp.float32)
    grad_w_down = jnp.einsum("rcf,rcd->fd", hidden_b, cotangent, preferred_element_type=jnp.float32)
    grad_b_down = jnp.sum(grad_out, axis=(0, 1))
    grad_hidden = jnp.einsum("rcd,fd->rcf", cotangent, w_down, preferred_element_type=jnp.float32)
    (grad_pre,) = gelu_pull(grad_hidden)
    grad_pre_b = grad_pre.astype(jnp.bfloat16)
    grad_w_up = jnp.einsum(
        "rcd,rcf->df", normed_two, grad_pre_b, preferred_element_type=jnp.float32
    )
    grad_b_up = jnp.sum(grad_pre_b.astype(jnp.float32), axis=(0, 1))
    grad_normed_two = jnp.einsum(
        "rcf,df->rcd", grad_pre_b, w_up, preferred_element_type=jnp.float32
    )
    grad_mid_norm, grad_ln2_gain, grad_ln2_bias = second_pull(grad_normed_two)
    grad_middle = grad_out + grad_mid_norm
    grad_branch_b = grad_middle.astype(jnp.bfloat16)
    grad_w_o = jnp.einsum("rce,rcd->ed", attn_b, grad_branch_b, preferred_element_type=jnp.float32)
    grad_b_o = jnp.sum(grad_branch_b.astype(jnp.float32), axis=(0, 1))
    grad_attn_b = jnp.einsum(
        "rcd,ed->rce", grad_branch_b, w_o, preferred_element_type=jnp.float32
    ).astype(jnp.bfloat16)
    delta_sum = jnp.sum((grad_attn_b.astype(jnp.float32) * attn_f32).reshape(head_shape), axis=-1)
    grad_heads = grad_attn_b.reshape(head_shape)
    whole_shape = (row_count, full_length, HEADS, head_size)
    back_state = (
        jnp.zeros(head_shape, jnp.float32),
        jnp.zeros(whole_shape, jnp.float32),
        jnp.zeros(whole_shape, jnp.float32),
    )
    backward_key_piece = lax.all_gather(key_b, "blk", axis=1, tiled=True)
    backward_value_piece = lax.all_gather(value_b, "blk", axis=1, tiled=True)

    def backward_block_step(block_index, inner_state):
        key_pos = block_index * slice_len + offsets
        key_seg = segment_of(cell_ends, key_pos)
        key_heads = take_block(backward_key_piece, block_index)
        value_heads = take_block(backward_value_piece, block_index)

        def backward_update(old_state):
            grad_query, grad_key, grad_value = backward_block(
                query_heads,
                grad_heads,
                log_total,
                delta_sum,
                key_heads,
                value_heads,
                query_pos,
                key_pos,
                query_seg,
                key_seg,
                scale_qk,
            )
            at_row = block_index * slice_len
            return (
                old_state[0] + grad_query,
                lax.dynamic_update_slice_in_dim(old_state[1], grad_key, at_row, 1),
                lax.dynamic_update_slice_in_dim(old_state[2], grad_value, at_row, 1),
            )

        return lax.cond(
            block_active(query_pos, key_pos, query_seg, key_seg),
            backward_update,
            unchanged,
            inner_state,
        )

    back_result = lax.fori_loop(
        0, backward_key_piece.shape[1] // slice_len, backward_block_step, back_state
    )
    grad_query_sum = back_result[0]
    grad_key_sum, grad_value_sum = (
        lax.psum_scatter(
            back_result[1].astype(jnp.bfloat16), "blk", scatter_dimension=1, tiled=True
        ).astype(jnp.float32),
        lax.psum_scatter(
            back_result[2].astype(jnp.bfloat16), "blk", scatter_dimension=1, tiled=True
        ).astype(jnp.float32),
    )
    flat_shape = (row_count, slice_len, width_all)
    grad_qkv_b = jnp.concatenate(
        [
            grad_query_sum.reshape(flat_shape),
            grad_key_sum.reshape(flat_shape),
            grad_value_sum.reshape(flat_shape),
        ],
        axis=-1,
    ).astype(jnp.bfloat16)
    grad_w_qkv = jnp.einsum(
        "rcd,rce->de", normed_one, grad_qkv_b, preferred_element_type=jnp.float32
    )
    column_sums = jnp.sum(grad_qkv_b.astype(jnp.float32), axis=(0, 1))
    grad_b_qv = jnp.concatenate([column_sums[:width_all], column_sums[2 * width_all :]])
    grad_normed_one = jnp.einsum(
        "rce,de->rcd", grad_qkv_b, w_qkv, preferred_element_type=jnp.float32
    )
    grad_in_norm, grad_ln1_gain, grad_ln1_bias = first_pull(grad_normed_one)
    input_grad = grad_middle + grad_in_norm
    grads = (
        grad_ln1_gain,
        grad_ln1_bias,
        grad_w_qkv,
        grad_b_qv,
        grad_w_o,
        grad_b_o,
        grad_ln2_gain,
        grad_ln2_bias,
        grad_w_up,
        grad_b_up,
        grad_w_down,
        grad_b_down,
    )
    summed = lax.psum(
        (
            grads[0],
            grads[1],
            grads[2],
            grads[3],
            grads[4],
            grads[5],
            grads[6],
            grads[7],
            grads[8],
            grads[9],
            grads[10],
            grads[11],
        ),
        ("rows", "blk"),
    )
    return (
        output,
        input_grad,
        summed[0],
        summed[1],
        summed[2],
        summed[3],
        summed[4],
        summed[5],
        summed[6],
        summed[7],
        summed[8],
        summed[9],
        summed[10],
        summed[11],
    )


def solution(mesh):
    in_specs = (
        P("rows", "blk", None),
        P("rows", None),
        P(),
        P(),
        P(),
        P(),
        P(),
        P(),
        P(),
        P(),
        P(),
        P(),
        P(),
        P(),
        P("rows", "blk", None),
    )
    out_specs = (
        P("rows", "blk", None),
        P("rows", "blk", None),
        P(),
        P(),
        P(),
        P(),
        P(),
        P(),
        P(),
        P(),
        P(),
        P(),
        P(),
        P(),
    )
    return jax.shard_map(
        per_device, mesh=mesh, in_specs=in_specs, out_specs=out_specs, check_vma=False
    )
```

profile of v0, /device:TPU:1, one launch (start us, length us, event | category | flops | bytes accessed | tf_op | source)
XLA Modules:
  0.0 572.3 jit_solution(14566362360158853154)
XLA Ops:
  16.6 2.7 slice.119
  21.3 32.4 %all-gather.5.cloned.1.call-done = bf16[4,1024,512]{2,1,0:T(8,128)(2,1)} async-done(((bf16[4,256,512]{2,1,0:T(8,128)(2,1)}), bf16[4,1024,512]{2,1,0:T(8,128)(2,1)}) %all-gather.5.cloned.1.call-update) | async-done | bytes 4194320 | tf_op jit(solution)/shard_map/all_gather | solution.py:128
  53.7 6.4 %copy.73 = bf16[4,1024,512]{1,2,0:T(8,128)(2,1)} copy(bf16[4,1024,512]{2,1,0:T(8,128)(2,1)} %all-gather.5.cloned.1.call-done) | data formatting | bytes 8388608
  60.0 30.3 %all-gather.3.cloned.1.call-done = bf16[4,1024,512]{2,1,0:T(8,128)(2,1)} async-done(((bf16[4,256,512]{2,1,0:T(8,128)(2,1)}), bf16[4,1024,512]{2,1,0:T(8,128)(2,1)}) %all-gather.3.cloned.1.call-update) | async-done | bytes 4194320 | tf_op jit(solution)/shard_map/all_gather | solution.py:127
  90.3 6.4 %copy.72 = bf16[4,1024,512]{1,2,0:T(8,128)(2,1)} copy(bf16[4,1024,512]{2,1,0:T(8,128)(2,1)} %all-gather.3.cloned.1.call-done) | data formatting | bytes 8388608
  98.3 34.9 %while.36 = (s32[]{:T(128)}, f32[4,256,8]{1,2,0:T(8,128)S(1)}, f32[4,256,8]{1,2,0:T(8,128)S(1)}, f32[4,256,8,64]{1,3,2,0:T(8,128)}, s32[256]{0:T(256)S(1)}, /*in...) while((s32[]{:T(128)}, f32[4,256,8]{1,2,0:T(8,128)S(1)}, ...), condition=%wide.region_11.12_spmd.clone, body=%wide.region_4.11_spmd.clone.sunk | while | flops 565812480 | bytes 55198256 | solution.py:160
  102.1 9.7 %conditional.6 = ((f32[4,256,8]{1,2,0:T(8,128)S(1)}, f32[4,256,8]{1,2,0:T(8,128)S(1)}, f32[4,256,8,64]{1,3,2,0:T(8,128)})) conditional(s32[]{:T(128)} %convert_element_type.215, (f32[4,256,8]{1,2,0:T(8,128)S(1)}, f32[4,256,8]{1,2,0:T(8,128)S(1)}, f32[4,256,8,64]{1,3,2,0:T(8,128)}) %tuple.121, (s32[256]{0:T(256)S(1)}, s32[256]{0:T(256)S(1)}, ...), branch_computations={%region_7.7_spmd, %region_8.10_spmd} | conditional | flops 565788672 | bytes 55191676 | solution.py:153
  115.7 9.7 %conditional.6 = ((f32[4,256,8]{1,2,0:T(8,128)S(1)}, f32[4,256,8]{1,2,0:T(8,128)S(1)}, f32[4,256,8,64]{1,3,2,0:T(8,128)})) conditional(s32[]{:T(128)} %convert_element_type.215, (f32[4,256,8]{1,2,0:T(8,128)S(1)}, f32[4,256,8]{1,2,0:T(8,128)S(1)}, f32[4,256,8,64]{1,3,2,0:T(8,128)}) %tuple.121, (s32[256]{0:T(256)S(1)}, s32[256]{0:T(256)S(1)}, ...), branch_computations={%region_7.7_spmd, %region_8.10_spmd} | conditional | flops 565788672 | bytes 55191676 | solution.py:153
  121.5 2.6 bitcast_add_fusion
  133.2 3.2 broadcast_divide_fusion
  136.4 2.9 copy.76
  139.3 2.7 fusion.77
  145.6 4.6 convert_reduce_fusion.3
  158.3 2.9 copy.77
  171.8 50.2 %while.37 = (s32[]{:T(128)}, f32[4,256,8,64]{1,3,2,0:T(8,128)}, bf16[4,1024,8,64]{1,3,2,0:T(8,128)(2,1)}, bf16[4,1024,8,64]{1,3,2,0:T(8,128)(2,1)}, s32[256]{0:T...) while((s32[]{:T(128)}, f32[4,256,8,64]{1,3,2,0:T(8,128)}, ...), condition=%wide.region_22.23_spmd.clone, body=%wide.region_17.22_spmd.clone.sunk | while | flops 1369529600 | bytes 146785072 | solution.py:241
  175.7 17.4 %conditional.7 = ((f32[4,256,8,64]{1,3,2,0:T(8,128)}, bf16[4,1024,8,64]{1,3,2,0:T(8,128)(2,1)}, bf16[4,1024,8,64]{1,3,2,0:T(8,128)(2,1)})) conditional(s32[]{:T(128)} %convert_element_type.217, (f32[4,256,8,64]{1,3,2,0:T(8,128)}, bf16[4,1024,8,64]{1,3,2,0:T(8,128)(2,1)}, bf16[4,1024,8,64]{1,3,2,0:T(8,128)(2,1)}) %tuple.124, (s32[256]{0:T(256)S(1)}, ...), branch_computations={%region_20.20_spmd, %region_21.21_spmd} | conditional | flops 1369505792 | bytes 146778432 | solution.py:234
  179.1 3.2 fusion.16
  182.4 3.5 bitcast_dynamic-update-slice_fusion
  196.9 17.4 %conditional.7 = ((f32[4,256,8,64]{1,3,2,0:T(8,128)}, bf16[4,1024,8,64]{1,3,2,0:T(8,128)(2,1)}, bf16[4,1024,8,64]{1,3,2,0:T(8,128)(2,1)})) conditional(s32[]{:T(128)} %convert_element_type.217, (f32[4,256,8,64]{1,3,2,0:T(8,128)}, bf16[4,1024,8,64]{1,3,2,0:T(8,128)(2,1)}, bf16[4,1024,8,64]{1,3,2,0:T(8,128)(2,1)}) %tuple.124, (s32[256]{0:T(256)S(1)}, ...), branch_computations={%region_20.20_spmd, %region_21.21_spmd} | conditional | flops 1369505792 | bytes 146778432 | solution.py:234
  200.3 3.2 fusion.16
  203.6 3.5 bitcast_dynamic-update-slice_fusion
  222.7 2.8 convert.12
  228.0 3.4 convolution_bitcast_fusion.3
  231.4 2.8 convolution_bitcast_fusion.2
  234.3 3.2 convolution_bitcast_fusion.1
  237.5 82.7 %reduce-scatter.5.cloned.1.call-done = bf16[4,256,8,64]{1,3,2,0:T(8,128)(2,1)} async-done(((bf16[4,1024,8,64]{1,3,2,0:T(8,128)(2,1)}), bf16[4,256,8,64]{1,3,2,0:T(8,128)(2,1)}) %reduce-scatter.5.cloned.1.call-update) | async-done | bytes 1048592 | tf_op jit(solution)/shard_map/reduce_scatter | solution.py:249
  322.5 44.7 %reduce-scatter.3.cloned.1.call-done = bf16[4,256,8,64]{1,3,2,0:T(8,128)(2,1)} async-done(((bf16[4,1024,8,64]{1,3,2,0:T(8,128)(2,1)}), bf16[4,256,8,64]{1,3,2,0:T(8,128)(2,1)}) %reduce-scatter.3.cloned.1.call-update) | async-done | bytes 1048592 | tf_op jit(solution)/shard_map/reduce_scatter | solution.py:246
  369.5 5.5 convolution_bitcast_fusion
  375.7 6.0 %add_convert_fusion = bf16[4,256,512]{2,1,0:T(8,128)(2,1)} fusion(f32[4,256,512]{2,1,0:T(8,128)} %copy-done.7, bf16[1024,512]{1,0:T(8,128)(2,1)} %param.35, f32[512]{0:T(512)S(1)} %copy-done.51, f32[4,256,1024]{2,1,0:T(8,128)} %copy-done.52, f32[1024]{0:T(1024)S(1)} %copy-done.47), kind=kOutput, calls=%fused_computation.91 | convolution fusion | flops 1085800448 | bytes 8394752 | tf_op jit(solution)/shard_map/dot_general | solution.py:173
  388.3 41.1 %all-reduce = (f32[512]{0:T(512)}, f32[512]{0:T(512)}, f32[1024]{0:T(1024)}, f32[512]{0:T(512)}, f32[512]{0:T(512)}, /*index=5*/f32[512]{0:T(512)}, f32[1024]{0:T(1024)}, f32[512]{0:T(512)}) all-reduce(f32[512]{0:T(512)S(1)} %get-tuple-element.876, f32[512]{0:T(512)S(1)} %get-tuple-element.879, ...), channel_id=1, replica_groups=mesh['rows'=8,'blk'=4] {'rows','blk'}, use_global_device_ids=true, to_apply=%region_28.29 | all-reduce | flops 5120 | bytes 40960 | tf_op jit(solution)/shard_map/psum | solution.py:286
  429.4 126.5 %all-reduce.4.cloned.1.call-done = (f32[512,1536]{1,0:T(8,128)}, f32[512,512]{1,0:T(8,128)}, f32[512,1024]{1,0:T(8,128)}, f32[1024,512]{1,0:T(8,128)}) async-done(((f32[512,1536]{1,0:T(8,128)}, f32[512,512]{1,0:T(8,128)}, f32[512,1024]{1,0:T(8,128)}, f32[1024,512]{1,0:T(8,128)}), (f32[512,1536]{1,0:T(8,128)}, f32[512,512]{1,0:T(8,128)}, f32[512,1024]{1,0:T(8,128)}, ...) | async-done | bytes 8388624 | tf_op jit(solution)/shard_map/psum | solution.py:286
  555.9 3.8 copy.138
  (257 shorter events, 108.4 us)
Async XLA Ops:
  7.2 4.0 copy-start
  7.2 4.0 copy-start.3
  7.2 4.0 copy-start.39
  7.2 4.0 copy-start.36
  7.2 4.0 copy-start.49
  7.2 46.4 %all-gather.5.cloned.1.call-start = ((), (), s32[]{:S(2)}) async-start(), calls=%async_computation.3 | async-start | bytes 5242880 | tf_op jit(solution)/shard_map/all_gather | solution.py:128
  8.9 4.2 copy-start.30
  13.2 3.4 copy-start.18
  16.6 73.8 %all-gather.3.cloned.1.call-start = ((), (), s32[]{:S(2)}) async-start(), calls=%async_computation.2 | async-start | bytes 5242880 | tf_op jit(solution)/shard_map/all_gather | solution.py:127
  19.3 300.8 %reduce-scatter.5.cloned.1.call-start = ((), (), s32[]{:S(2)}) async-start(), calls=%async_computation.5 | async-start | bytes 5242880 | tf_op jit(solution)/shard_map/reduce_scatter | solution.py:249
  142.0 10.5 %copy-start.7 = (f32[4,256,512]{2,1,0:T(8,128)}, f32[4,256,512]{2,1,0:T(8,128)S(1)}, u32[]{:S(2)}) copy-start(f32[4,256,512]{2,1,0:T(8,128)S(1)} %get-tuple-element.960) | copy-start | bytes 6291460
  145.6 4.6 copy-start.52
  154.7 3.6 copy-start.13
  182.4 3.5 copy-start.1
  185.9 3.7 copy-start.11
  200.3 3.3 copy-start.9
  203.6 3.5 copy-start.1
  207.1 3.7 copy-start.11
  222.1 145.2 %reduce-scatter.3.cloned.1.call-start = ((), (), s32[]{:S(2)}) async-start(), calls=%async_computation.4 | async-start | bytes 5242880 | tf_op jit(solution)/shard_map/reduce_scatter | solution.py:246
  222.6 333.2 %all-reduce.4.cloned.1.call-start = ((), (), s32[]{:S(2)}) async-start(), calls=%async_computation.6 | async-start | bytes 16777216 | tf_op jit(solution)/shard_map/psum | solution.py:286
  222.7 5.3 copy-start.14
  228.0 3.4 copy-start.8
  228.0 3.4 copy-start.55
  320.2 49.3 %copy-start.4 = (bf16[4,256,512]{2,1,0:T(8,128)(2,1)S(1)}, bf16[4,256,512]{2,1,0:T(8,128)(2,1)}, u32[]{:S(2)}) copy-start(bf16[4,256,512]{2,1,0:T(8,128)(2,1)} %param.23) | copy-start | bytes 3145732
  320.2 49.3 %copy-start.31 = (f32[4,256]{1,0:T(4,128)S(1)}, f32[4,256]{1,0:T(4,128)}, u32[]{:S(2)}) copy-start(f32[4,256]{1,0:T(4,128)} %copy-done.30) | copy-start | bytes 12292
  320.2 49.3 %copy-start.33 = (f32[4,256]{1,0:T(4,128)S(1)}, f32[4,256]{1,0:T(4,128)}, u32[]{:S(2)}) copy-start(f32[4,256]{1,0:T(4,128)} %copy-done.32) | copy-start | bytes 12292
  320.2 49.3 %copy-start.37 = (f32[512]{0:T(512)S(1)}, f32[512]{0:T(512)}, u32[]{:S(2)}) copy-start(f32[512]{0:T(512)} %param.25) | copy-start | bytes 6148
  320.2 49.4 %copy-start.50 = (f32[512]{0:T(512)S(1)}, f32[512]{0:T(512)}, u32[]{:S(2)}) copy-start(f32[512]{0:T(512)} %param.26) | copy-start | bytes 6148
  375.7 6.0 %copy-start.22 = (bf16[4,256,512]{2,1,0:T(8,128)(2,1)S(1)}, bf16[4,256,512]{2,1,0:T(8,128)(2,1)}, u32[]{:S(2)}) copy-start(bf16[4,256,512]{2,1,0:T(8,128)(2,1)} %copy.80) | copy-start | bytes 3145732
  375.7 6.0 %copy-start.23 = (bf16[4,256,512]{2,1,0:T(8,128)(2,1)S(1)}, bf16[4,256,512]{2,1,0:T(8,128)(2,1)}, u32[]{:S(2)}) copy-start(bf16[4,256,512]{2,1,0:T(8,128)(2,1)} %copy.82) | copy-start | bytes 3145732
  375.7 6.0 %copy-start.24 = (bf16[4,256,512]{2,1,0:T(8,128)(2,1)S(1)}, bf16[4,256,512]{2,1,0:T(8,128)(2,1)}, u32[]{:S(2)}) copy-start(bf16[4,256,512]{2,1,0:T(8,128)(2,1)} %copy.81) | copy-start | bytes 3145732
  555.9 3.8 copy-start.29
  (38 other events, 73.0 us)
Sparse Core Ops, SparseCore 0:
  16.7 36.9 all-gather.4
  55.8 34.4 all-gather.2
  222.2 97.9 reduce-scatter.4
  322.7 44.4 reduce-scatter.2
  375.2 180.6 all-reduce.3
where the time goes:
time: 577 us; the launch traced here: 572 us
  waiting for transfers between devices  317 us (55%)
  local copies, waits for them, and re-layouts  84.4 us (15%)
  matrix products  67.2 us (12%)
  blocking collectives  41.1 us (7%)
  other arithmetic  31.1 us (5%)
  loops' own time  16.3 us (3%)
  between operations  14.7 us (3%)
    psum x1, waiting for transfers between devices, per_device(): lax.psum((grads[0], grads[1], grads[2], grads[3], grads[4], grads[5], gra...  126 us
    reduce_scatter x1, waiting for transfers between devices, per_device(): lax.psum_scatter(back_result[2].astype(jnp.bfloat16), 'blk', scatter_dime...  82.7 us
    reduce_scatter x1, waiting for transfers between devices, per_device(): lax.psum_scatter(back_result[1].astype(jnp.bfloat16), 'blk', scatter_dime...  44.7 us
    psum x1, blocking collectives, per_device(): lax.psum((grads[0], grads[1], grads[2], grads[3], grads[4], grads[5], gra...  41.1 us
    all_gather x1, waiting for transfers between devices, per_device(): value_piece = lax.all_gather(value_b, 'blk', axis=1, tiled=True)  32.4 us
    all_gather x1, waiting for transfers between devices, per_device(): key_piece = lax.all_gather(key_b, 'blk', axis=1, tiled=True)  30.3 us
    unnamed x100, local copies, waits for them, and re-layouts  29 us
    cond x38, local copies, waits for them, and re-layouts  12.3 us
  transfers between devices with their start and end apart: 5, of which 5 were waited for; matrix products, arithmetic and copies ran while one was open for 7% of the time, Pallas kernels for 0%

commit v1 on v0

--- a/solution.py
+++ b/solution.py
@@ -1,13 +1,477 @@
+import functools
+
 import jax
 import jax.numpy as jnp
 from jax import lax
+from jax.experimental import pallas as pl
+from jax.experimental.pallas import tpu as pltpu
 from jax.sharding import PartitionSpec as P
 
 HEADS = 8
-
-
 norm_eps = 1e-05
 neg_big = -1e30
+BOTH = ("rows", "blk")
+F32 = jnp.float32
+BF16 = jnp.bfloat16
+TILE = 256
+LANES = 128
+VMEM_LIMIT = 56 * 1024 * 1024
+
+
+def mm(lhs, rhs):
+    return lax.dot_general(lhs, rhs, (((1,), (0,)), ((), ())), preferred_element_type=F32)
+
+
+def mm_nt(lhs, rhs):
+    return lax.dot_general(lhs, rhs, (((1,), (1,)), ((), ())), preferred_element_type=F32)
+
+
+def mm_tn(lhs, rhs):
+    return lax.dot_general(lhs, rhs, (((0,), (0,)), ((), ())), preferred_element_type=F32)
+
+
+def cell_start(ends_ref, positions):
+    start = jnp.zeros_like(positions)
+    for c in range(ends_ref.shape[0]):
+        start = jnp.where(ends_ref[c] <= positions, ends_ref[c], start)
+    return start
+
+
+def norm_parts(values):
+    average = jnp.mean(values, axis=-1, keepdims=True)
+    centered = values - average
+    variance = jnp.mean(centered * centered, axis=-1, keepdims=True)
+    scale = lax.rsqrt(variance + norm_eps)
+    return centered * scale, scale
+
+
+def norm_pull(e, n, scale, gain):
+    f = e * gain
+    return (
+        f
+        - jnp.mean(f, axis=-1, keepdims=True)
+        - n * jnp.mean(f * n, axis=-1, keepdims=True)
+    ) * scale
+
+
+def head_lanes(shape, half):
+    lane = lax.broadcasted_iota(jnp.int32, shape, len(shape) - 1)
+    return (lane < LANES // 2) if half == 0 else (lane >= LANES // 2)
+
+
+def only_head(values, half):
+    return jnp.where(head_lanes(values.shape, half), values, jnp.zeros_like(values))
+
+
+def forward_kernel(
+    ends_ref, x_ref, gain_ref, bias_ref, w_ref, b_ref,
+    q_ref, k_ref, v_ref, n1_ref, att_ref, lse_ref,
+    mask_ref,
+):
+    i = pl.program_id(0)
+    tiles = pl.num_programs(0)
+    del tiles
+    width = x_ref.shape[-1]
+    pairs = width // LANES
+    scale_qk = (width // HEADS) ** (-0.5)
+    n, _ = norm_parts(x_ref[...].astype(F32))
+    n1 = (n * gain_ref[...] + bias_ref[...]).astype(BF16)
+    n1_ref[...] = n1
+    rows = pl.ds(pl.multiple_of(i * TILE, TILE), TILE)
+    q = mm(n1, w_ref[:, :width]) + b_ref[:, :width]
+    q = (q.astype(BF16).astype(F32) * scale_qk).astype(BF16)
+    k = mm(n1, w_ref[:, width : 2 * width]).astype(BF16)
+    v = (mm(n1, w_ref[:, 2 * width :]) + b_ref[:, width:]).astype(BF16)
+    for g in range(pairs):
+        cols = slice(g * LANES, (g + 1) * LANES)
+        q_ref[g] = q[:, cols]
+        k_ref[g, rows, :] = k[:, cols]
+        v_ref[g, rows, :] = v[:, cols]
+
+    def attend(tile):
+        reach = (tile + 1) * TILE
+        q_pos = tile * TILE + lax.broadcasted_iota(jnp.int32, (TILE, 1), 0)
+        k_pos = lax.broadcasted_iota(jnp.int32, (TILE, reach), 1)
+        start = cell_start(ends_ref, q_pos)
+        mask_ref[:, :reach] = jnp.where((k_pos <= q_pos) & (k_pos >= start), 0.0, neg_big)
+
+        def one_pair(g, lse_all):
+            qp = q_ref[g]
+            kp = k_ref[g, :reach, :]
+            vp = v_ref[g, :reach, :]
+            outs = []
+            for half in range(2):
+                s = mm_nt(only_head(qp, half), kp) + mask_ref[:, :reach]
+                top = jnp.max(s, axis=-1, keepdims=True)
+                p = jnp.exp(s - top)
+                total = jnp.sum(p, axis=-1, keepdims=True)
+                outs.append(mm(p.astype(BF16), vp) / total)
+                lse = top + jnp.log(total)
+                lane = lax.broadcasted_iota(jnp.int32, lse_all.shape, 1)
+                lse_all = jnp.where(lane == 2 * g + half, lse, lse_all)
+            att_ref[g] = jnp.where(head_lanes(outs[0].shape, 0), outs[0], outs[1])
+            return lse_all
+
+        lse_all = lax.fori_loop(0, pairs, one_pair, jnp.zeros((TILE, LANES), F32))
+        lse_ref[...] = jnp.transpose(lse_all)[:HEADS]
+
+    for tile in range(k_ref.shape[1] // TILE):
+        pl.when(i == tile)(functools.partial(attend, tile))
+
+
+def whole(shape):
+    return pl.BlockSpec(shape, lambda i: (0,) * len(shape))
+
+
+def by_row(cols):
+    return pl.BlockSpec((TILE, cols), lambda i: (i, 0))
+
+
+def by_pair(pairs):
+    return pl.BlockSpec((pairs, TILE, LANES), lambda i: (0, i, 0))
+
+
+def heads_row():
+    return pl.BlockSpec((HEADS, TILE), lambda i: (0, i))
+
+
+SMEM_SPEC = pl.BlockSpec(memory_space=pltpu.SMEM)
+
+
+def params():
+    return pltpu.CompilerParams(
+        dimension_semantics=("arbitrary",), vmem_limit_bytes=VMEM_LIMIT
+    )
+
+
+def cost(flops, moved):
+    return pl.CostEstimate(flops=int(flops), bytes_accessed=int(moved), transcendentals=0)
+
+
+def forward_call(ends, x, gain, bias, w_qkv, b_qv):
+    t, d = x.shape
+    pairs = d // LANES
+    return pl.pallas_call(
+        forward_kernel,
+        grid=(t // TILE,),
+        in_specs=[
+            SMEM_SPEC, by_row(d), whole((1, d)), whole((1, d)), whole(w_qkv.shape), whole((1, 2 * d)),
+        ],
+        out_specs=[
+            by_pair(pairs), whole((pairs, t, LANES)), whole((pairs, t, LANES)), by_row(d),
+            by_pair(pairs), heads_row(),
+        ],
+        out_shape=[
+            jax.ShapeDtypeStruct((pairs, t, LANES), BF16),
+            jax.ShapeDtypeStruct((pairs, t, LANES), BF16),
+            jax.ShapeDtypeStruct((pairs, t, LANES), BF16),
+            jax.ShapeDtypeStruct((t, d), BF16),
+            jax.ShapeDtypeStruct((pairs, t, LANES), F32),
+            jax.ShapeDtypeStruct((HEADS, t), F32),
+        ],
+        scratch_shapes=[pltpu.VMEM((TILE, t), F32)],
+        compiler_params=params(),
+        cost_estimate=cost(15e9, 10e6),
+        name="forward",
+    )(ends, x, gain[None], bias[None], w_qkv, b_qv[None])
+
+
+def middle_kernel(
+    att_ref, x_ref, cot_ref, wo_ref, bo_ref, gain_ref, bias_ref, wup_ref, bup_ref, wdown_ref, bdown_ref,
+    out_ref, gmid_ref, gatt_ref, delta_ref, gwdown_ref, gwup_ref, gwo_ref, vec_ref,
+):
+    i = pl.program_id(0)
+    pairs = att_ref.shape[0]
+    d = x_ref.shape[-1]
+    ff = wup_ref.shape[-1]
+
+    @pl.when(i == 0)
+    def _():
+        gwdown_ref[...] = jnp.zeros_like(gwdown_ref)
+        gwup_ref[...] = jnp.zeros_like(gwup_ref)
+        gwo_ref[...] = jnp.zeros_like(gwo_ref)
+        vec_ref[...] = jnp.zeros_like(vec_ref)
+
+    att = jnp.concatenate([att_ref[g] for g in range(pairs)], axis=-1)
+    att_b = att.astype(BF16)
+    middle = x_ref[...].astype(F32) + mm(att_b, wo_ref[...]) + bo_ref[...]
+    n, scale = norm_parts(middle)
+    n2 = (n * gain_ref[...] + bias_ref[...]).astype(BF16)
+    pre = mm(n2, wup_ref[...]) + bup_ref[...]
+    c0 = 0.7978845608028654
+    c1 = 0.044715
+    sq = pre * pre
+    t = jnp.tanh(c0 * (pre + c1 * (sq * pre)))
+    half_one = 0.5 * (1.0 + t)
+    hidden = (pre * half_one).astype(BF16)
+    slope = half_one + (0.5 * pre) * (1.0 - t * t) * (c0 + (3.0 * c0 * c1) * sq)
+    out_ref[...] = (middle + mm(hidden, wdown_ref[...]) + bdown_ref[...]).astype(BF16)
+
+    cot = cot_ref[...]
+    cot_f = cot.astype(F32)
+    gwdown_ref[...] += mm_tn(hidden, cot)
+    gpre = (mm_nt(cot, wdown_ref[...]) * slope).astype(BF16)
+    gwup_ref[...] += mm_tn(n2, gpre)
+    e = mm_nt(gpre, wup_ref[...])
+    gmid = cot_f + norm_pull(e, n, scale, gain_ref[...])
+    gmid_ref[...] = gmid
+    gbr = gmid.astype(BF16)
+    gwo_ref[...] += mm_tn(att_b, gbr)
+    gatt = mm_nt(gbr, wo_ref[...]).astype(BF16)
+    for g in range(pairs):
+        gatt_ref[g] = gatt[:, g * LANES : (g + 1) * LANES]
+    prod = gatt.astype(F32) * att
+    hi = prod.astype(BF16)
+    lo = (prod - hi.astype(F32)).astype(BF16)
+    head = lax.broadcasted_iota(jnp.int32, (HEADS, d), 0)
+    lane = lax.broadcasted_iota(jnp.int32, (HEADS, d), 1)
+    ones = jnp.where(lane // (d // HEADS) == head, 1.0, 0.0).astype(BF16)
+    delta_ref[...] = mm_nt(ones, hi) + mm_nt(ones, lo)
+
+    def col(values):
+        return jnp.sum(values, axis=0, keepdims=True)
+
+    gsum = col(gpre.astype(F32))
+    vec_ref[0:1] += col(cot_f)
+    vec_ref[1:2] += gsum[:, :d]
+    vec_ref[2:3] += gsum[:, d:]
+    vec_ref[3:4] += col(e * n)
+    vec_ref[4:5] += col(e)
+    vec_ref[5:6] += col(gbr.astype(F32))
+
+
+def middle_call(att, x, cot, w_o, b_o, gain, bias, w_up, b_up, w_down, b_down):
+    t, d = x.shape
+    pairs = d // LANES
+    ff = w_up.shape[1]
+    return pl.pallas_call(
+        middle_kernel,
+        grid=(t // TILE,),
+        in_specs=[
+            by_pair(pairs), by_row(d), by_row(d), whole((d, d)), whole((1, d)), whole((1, d)), whole((1, d)),
+            whole((d, ff)), whole((1, ff)), whole((ff, d)), whole((1, d)),
+        ],
+        out_specs=[
+            by_row(d), by_row(d), by_pair(pairs), heads_row(), whole((ff, d)), whole((d, ff)),
+            whole((d, d)), whole((8, d)),
+        ],
+        out_shape=[
+            jax.ShapeDtypeStruct((t, d), BF16),
+            jax.ShapeDtypeStruct((t, d), F32),
+            jax.ShapeDtypeStruct((pairs, t, LANES), BF16),
+            jax.ShapeDtypeStruct((HEADS, t), F32),
+            jax.ShapeDtypeStruct((ff, d), F32),
+            jax.ShapeDtypeStruct((d, ff), F32),
+            jax.ShapeDtypeStruct((d, d), F32),
+            jax.ShapeDtypeStruct((8, d), F32),
+        ],
+        compiler_params=params(),
+        cost_estimate=cost(15e9, 20e6),
+        name="middle",
+    )(att, x, cot, w_o, b_o[None], gain[None], bias[None], w_up, b_up[None], w_down, b_down[None])
+
+
+def backward_kernel(first, ends_ref, q_ref, k_ref, v_ref, g_ref, lse_ref, delta_ref, dq_ref, dk_ref, dv_ref, acc_ref):
+    pair = pl.program_id(0) + first
+    t = q_ref.shape[1]
+    scale_qk = (LANES // 2) ** (-0.5)
+    pos_row = lax.broadcasted_iota(jnp.int32, (1, t), 1)
+    start_row = cell_start(ends_ref, pos_row)
+    acc_ref[...] = jnp.zeros_like(acc_ref)
+    for j in range(t // TILE):
+        low = j * TILE
+        kp = k_ref[0, low : low + TILE, :]
+        vp = v_ref[0, low : low + TILE, :]
+        qp = q_ref[0, low:, :]
+        gp = g_ref[0, low:, :]
+        k_pos = low + lax.broadcasted_iota(jnp.int32, (TILE, t - low), 0)
+        allowed = (k_pos >= start_row[:, low:]) & (k_pos <= pos_row[:, low:])
+        dks, dvs = [], []
+        for half in range(2):
+            lse = lse_ref[pl.ds(2 * pair + half, 1), low:]
+            delta = delta_ref[pl.ds(2 * pair + half, 1), low:]
+            km = only_head(kp, half)
+            s = mm_nt(km, qp)
+            p = jnp.exp(jnp.where(allowed, s - lse, neg_big))
+            dp = mm_nt(only_head(vp, half), gp)
+            ds = (p * (dp - delta)).astype(BF16)
+            dvs.append(mm(p.astype(BF16), gp))
+            dks.append(mm(ds, qp))
+            acc_ref[low:, :] += mm_tn(ds, km)
+        first_lanes = head_lanes(dks[0].shape, 0)
+        dk_ref[0, low : low + TILE, :] = jnp.where(first_lanes, dks[0], dks[1]).astype(BF16)
+        dv_ref[0, low : low + TILE, :] = jnp.where(first_lanes, dvs[0], dvs[1]).astype(BF16)
+    dq_ref[0] = (acc_ref[...] * scale_qk).astype(BF16)
+
+
+def backward_call(ends, q, k, v, gatt, lse, delta, first, count):
+    pairs, t, _ = q.shape
+    spec = pl.BlockSpec((1, t, LANES), lambda i: (i + first, 0, 0))
+    out = pl.BlockSpec((1, t, LANES), lambda i: (i, 0, 0))
+    return pl.pallas_call(
+        functools.partial(backward_kernel, first),
+        grid=(count,),
+        in_specs=[SMEM_SPEC, spec, spec, spec, spec, whole((HEADS, t)), whole((HEADS, t))],
+        out_specs=[out, out, out],
+        out_shape=[jax.ShapeDtypeStruct((count, t, LANES), BF16)] * 3,
+        scratch_shapes=[pltpu.VMEM((t, LANES), F32)],
+        compiler_params=params(),
+        cost_estimate=cost(count * 6e9, count * 3e6),
+        name="backward",
+    )(ends, q, k, v, gatt, lse, delta)
+
+
+def last_kernel(dq_ref, dk_ref, dv_ref, n1_ref, x_ref, gmid_ref, gain_ref, w_ref, gin_ref, gw_ref, vec_ref):
+    i = pl.program_id(0)
+    pairs = dq_ref.shape[0]
+    d = x_ref.shape[-1]
+
+    @pl.when(i == 0)
+    def _():
+        gw_ref[...] = jnp.zeros_like(gw_ref)
+        vec_ref[...] = jnp.zeros_like(vec_ref)
+
+    parts = [ref[g] for ref in (dq_ref, dk_ref, dv_ref) for g in range(pairs)]
+    gqkv = jnp.concatenate(parts, axis=-1)
+    gw_ref[...] += mm_tn(n1_ref[...], gqkv)
+    e = mm_nt(gqkv, w_ref[...])
+    n, scale = norm_parts(x_ref[...].astype(F32))
+    gin_ref[...] = (gmid_ref[...] + norm_pull(e, n, scale, gain_ref[...])).astype(BF16)
+
+    def col(values):
+        return jnp.sum(values, axis=0, keepdims=True)
+
+    vec_ref[0:1] += col(e * n)
+    vec_ref[1:2] += col(e)
+    vec_ref[2:3] += col(gqkv[:, :d].astype(F32))
+    vec_ref[3:4] += col(gqkv[:, 2 * d :].astype(F32))
+
+
+def last_call(dq, dk, dv, n1, x, gmid, gain, w_qkv):
+    t, d = x.shape
+    pairs = d // LANES
+    return pl.pallas_call(
+        last_kernel,
+        grid=(t // TILE,),
+        in_specs=[
+            by_pair(pairs), by_pair(pairs), by_pair(pairs), by_row(d), by_row(d), by_row(d),
+            whole((1, d)), whole(w_qkv.shape),
+        ],
+        out_specs=[by_row(d), whole((d, 3 * d)), whole((8, d))],
+        out_shape=[
+            jax.ShapeDtypeStruct((t, d), BF16),
+            jax.ShapeDtypeStruct((d, 3 * d), F32),
+            jax.ShapeDtypeStruct((8, d), F32),
+        ],
+        compiler_params=params(),
+        cost_estimate=cost(8e9, 12e6),
+        name="last",
+    )(dq, dk, dv, n1, x, gmid, gain[None], w_qkv)
+
+
+def device_bits():
+    count = lax.axis_size(BOTH)
+    me = lax.axis_index("rows") * lax.axis_size("blk") + lax.axis_index("blk")
+    return me, count
+
+
+def send_xor(values, flip):
+    count = lax.axis_size(BOTH)
+    return lax.ppermute(values, BOTH, [(i, i ^ flip) for i in range(count)])
+
+
+def piece(values, index, parts):
+    size = values.shape[0] // parts
+    return lax.dynamic_slice_in_dim(values, index * size, size, 0)
+
+
+def scatter_stage(values, shift, parts, me):
+    mine = (me >> shift) & (parts - 1)
+    total = piece(values, mine, parts)
+    for flip in range(1, parts):
+        sent = piece(values, mine ^ flip, parts).astype(BF16)
+        total = total + send_xor(sent, flip << shift).astype(F32)
+    return total
+
+
+def gather_stage(values, shift, parts, me):
+    mine = (me >> shift) & (parts - 1)
+    out = jnp.zeros((parts,) + values.shape, values.dtype)
+    out = lax.dynamic_update_slice_in_dim(out, values[None], mine, 0)
+    for flip in range(1, parts):
+        out = lax.dynamic_update_slice_in_dim(
+            out, send_xor(values, flip << shift)[None], mine ^ flip, 0
+        )
+    return out.reshape((parts * values.shape[0],) + values.shape[1:])
+
+
+STAGES = ((0, 2), (1, 4), (3, 4))
+
+
+def sum_all(values):
+    me, _ = device_bits()
+    for shift, parts in STAGES:
+        values = scatter_stage(values, shift, parts, me)
+    values = values.astype(BF16)
+    for shift, parts in reversed(STAGES):
+        values = gather_stage(values, shift, parts, me)
+    return values.astype(F32)
+
+
+def sum_small(values):
+    for shift, parts in STAGES:
+        total = values
+        for flip in range(1, parts):
+            total = total + send_xor(values, flip << shift)
+        values = total
+    return values
+
+
+def row_device(
+    tokens, seg_lengths, ln1_gain, ln1_bias, w_qkv, b_qv, w_o, b_o, ln2_gain, ln2_bias,
+    w_up, b_up, w_down, b_down, cotangent,
+):
+    row_count, slice_len, d = tokens.shape
+    t = row_count * slice_len
+    ff = w_up.shape[1]
+    row = lax.axis_index("blk")
+    ends = jnp.cumsum(seg_lengths, axis=1)
+    ends = lax.dynamic_index_in_dim(ends, row, 0, keepdims=False).astype(jnp.int32)
+
+    def swap(values):
+        return lax.all_to_all(values, "blk", 0, 0, tiled=True)
+
+    x = swap(tokens).reshape(t, d)
+    cot = swap(cotangent).reshape(t, d)
+    q, k, v, n1, att, lse = forward_call(ends, x, ln1_gain, ln1_bias, w_qkv, b_qv)
+    out, gmid, gatt, delta, gw_down, gw_up, gw_o, vec_mid = middle_call(
+        att, x, cot, w_o, b_o, ln2_gain, ln2_bias, w_up, b_up, w_down, b_down
+    )
+    output = swap(out.reshape(row_count, slice_len, d))
+    dq, dk, dv = backward_call(ends, q, k, v, gatt, lse, delta, 0, d // LANES)
+    gin, gw_qkv, vec_last = last_call(dq, dk, dv, n1, x, gmid, ln1_gain, w_qkv)
+    input_grad = swap(gin.reshape(row_count, slice_len, d)).astype(F32)
+    first = jnp.concatenate([gw_down, gw_up[:, :d], gw_up[:, d:], gw_o], axis=0)
+    first = sum_all(first)
+    second = jnp.concatenate([gw_qkv[:, :d], gw_qkv[:, d : 2 * d], gw_qkv[:, 2 * d :]], axis=0)
+    second = sum_all(second)
+    vec = sum_small(jnp.concatenate([vec_mid, vec_last], axis=0))
+    return (
+        output,
+        input_grad,
+        vec[8],
+        vec[9],
+        jnp.concatenate([second[:d], second[d : 2 * d], second[2 * d :]], axis=1),
+        jnp.concatenate([vec[10], vec[11]]),
+        first[ff + 2 * d :],
+        vec[5],
+        vec[3],
+        vec[4],
+        jnp.concatenate([first[ff : ff + d], first[ff + d : ff + 2 * d]], axis=1),
+        jnp.concatenate([vec[1], vec[2]]),
+        first[:ff],
+        vec[0],
+    )
 
 
 def layer_norm(values, gain_vec, bias_vec):
@@ -78,7 +542,7 @@
     return old_state
 
 
-def per_device(
+def general_device(
     tokens,
     seg_lengths,
     ln1_gain,
@@ -318,6 +782,17 @@
     )
 
 
+def device_function(tokens, *rest):
+    d = tokens.shape[2]
+    whole_rows = (
+        lax.axis_size("blk") == tokens.shape[0] == 4
+        and lax.axis_size("rows") == 8
+        and tokens.shape[1] == TILE
+        and d == 512
+    )
+    return (row_device if whole_rows else general_device)(tokens, *rest)
+
+
 def solution(mesh):
     in_specs = (
         P("rows", "blk", None),
@@ -353,5 +828,5 @@
         P(),
     )
     return jax.shard_map(
-        per_device, mesh=mesh, in_specs=in_specs, out_specs=out_specs, check_vma=False
-    )
+        device_function, mesh=mesh, in_specs=in_specs, out_specs=out_specs, check_vma=False
+    )

time: 577 us -> 222 us (0.38)
  waiting for transfers between devices: 317 us -> 56.5 us
  local copies, waits for them, and re-layouts: 84.4 us -> 16 us
  Pallas kernels: 0 us -> 68.1 us
  matrix products: 67.2 us -> 0 us
  starting transfers between devices: 0.37 us -> 64.3 us
  blocking collectives: 41.1 us -> 0 us
  other arithmetic: 31.1 us -> 14.7 us
  loops' own time: 16.3 us -> 0 us
  between operations: 14.7 us -> 1.15 us
    reduce_scatter x2 -> x0, waiting for transfers between devices: 127 us -> none  [the longest x1 82.7 us: per_device(): lax.psum_scatter(back_result[2].astype(jnp.bfloat16), 'blk', scatter_dime...]
    psum x1 -> x0, waiting for transfers between devices: 126 us -> none  [per_device(): lax.psum((grads[0], grads[1], grads[2], grads[3], grads[4], grads[5], gra...]
    pallas_call x0 -> x4, Pallas kernels: none -> 68.1 us  [the longest x1 21.8 us: forward_call(): pl.pallas_call(forward_kernel, grid=(t // TILE,), in_specs=[SMEM_SPEC, by...]
    dot_general x26 -> x0, matrix products: 67.2 us -> none  [the longest x2 7.01 us: backward_block(): jnp.einsum('rqhk,rqhd->rkhd', softmaxed.astype(jnp.bfloat16), grad_heads,...]
    all_gather x2 -> x0, waiting for transfers between devices: 62.7 us -> none  [the longest x1 32.4 us: per_device(): value_piece = lax.all_gather(value_b, 'blk', axis=1, tiled=True)]
    ppermute x0 -> x35, starting transfers between devices: none -> 46.4 us  [send_xor(): return lax.ppermute(values, BOTH, [(i, i ^ flip) for i in range(count)])]
    psum x1 -> x0, blocking collectives: 41.1 us -> none  [per_device(): lax.psum((grads[0], grads[1], grads[2], grads[3], grads[4], grads[5], gra...]
    ppermute x0 -> x35, waiting for transfers between devices: none -> 35.3 us  [send_xor(): return lax.ppermute(values, BOTH, [(i, i ^ flip) for i in range(count)])]
  transfers between devices with their start and end apart: 5 -> 39, of which waited for: 5 -> 14; matrix products, arithmetic and copies ran while one was open for 7% -> 9% of each run, Pallas kernels for 0% -> 10%
where the time goes in v1:
time: 222 us; the launch traced here: 221 us
  Pallas kernels  68.1 us (31%)
  starting transfers between devices  64.3 us (29%)
  waiting for transfers between devices  56.5 us (25%)
  local copies, waits for them, and re-layouts  16 us (7%)
  other arithmetic  14.7 us (7%)
    ppermute x35, starting transfers between devices, send_xor(): return lax.ppermute(values, BOTH, [(i, i ^ flip) for i in range(count)])  46.4 us
    ppermute x35, waiting for transfers between devices, send_xor(): return lax.ppermute(values, BOTH, [(i, i ^ flip) for i in range(count)])  35.3 us
    pallas_call x1, Pallas kernels, forward_call(): pl.pallas_call(forward_kernel, grid=(t // TILE,), in_specs=[SMEM_SPEC, by...  21.8 us
    all_to_all x4, waiting for transfers between devices, swap(): return lax.all_to_all(values, 'blk', 0, 0, tiled=True)  21.2 us
    pallas_call x1, Pallas kernels, middle_call(): pl.pallas_call(middle_kernel, grid=(t // TILE,), in_specs=[by_pair(pairs)...  19 us
    pallas_call x1, Pallas kernels, backward_call(): pl.pallas_call(functools.partial(backward_kernel, first), grid=(count,),...  18.6 us
    all_to_all x4, starting transfers between devices, swap(): return lax.all_to_all(values, 'blk', 0, 0, tiled=True)  18 us
    pallas_call x1, Pallas kernels, last_call(): pl.pallas_call(last_kernel, grid=(t // TILE,), in_specs=[by_pair(pairs),...  8.78 us
  transfers between devices with their start and end apart: 39, of which 14 were waited for; matrix products, arithmetic and copies ran while one was open for 9% of the time, Pallas kernels for 10%

profile of v1, /device:TPU:1, one launch (start us, length us, event | category | flops | bytes accessed | tf_op | source)
XLA Modules:
  0.0 220.7 jit_solution(16011944249725103195)
XLA Ops:
  0.7 4.3 %all-to-all-start = ((bf16[4,256,512]{2,1,0:T(8,128)(2,1)}), bf16[4,256,512]{2,1,0:T(8,128)(2,1)S(1)}, u32[]{:S(2)}, u32[]{:S(2)}) async-start(bf16[4,256,512]{2,1,0:T(8,128)(2,1)} %param.15), calls=%async_computation | async-start | bytes 2097152 | tf_op jit(solution)/shard_map/all_to_all | solution.py:442
  5.7 12.6 %all-to-all-done = bf16[4,256,512]{2,1,0:T(8,128)(2,1)S(1)} async-done(((bf16[4,256,512]{2,1,0:T(8,128)(2,1)}), bf16[4,256,512]{2,1,0:T(8,128)(2,1)S(1)}, u32[]{:S(2)}, u32[]{:S(2)}) %all-to-all-start) | async-done | bytes 1048608 | tf_op jit(solution)/shard_map/all_to_all | solution.py:442
  18.3 4.6 %all-to-all-start.1 = ((bf16[4,256,512]{2,1,0:T(8,128)(2,1)}), bf16[4,256,512]{2,1,0:T(8,128)(2,1)S(1)}, u32[]{:S(2)}, u32[]{:S(2)}) async-start(bf16[4,256,512]{2,1,0:T(8,128)(2,1)} %param.29), calls=%async_computation.1 | async-start | bytes 2097152 | tf_op jit(solution)/shard_map/all_to_all | solution.py:442
  22.9 21.8 %forward.1 = (bf16[4,1024,128]{2,1,0:T(8,128)(2,1)}, bf16[4,1024,128]{2,1,0:T(8,128)(2,1)}, bf16[4,1024,128]{2,1,0:T(8,128)(2,1)}, bf16[1024,512]{1,0:T(8,128)(2...) custom-call(s32[8]{0:T(128)} %fusion.ends_ref, bf16[1024,512]{1,0:T(8,128)(2,1)} %bitcast.86, f32[1,512]{1,0:T(1,128)} %bitcast.113, ...), custom_call_target="tpu_custom_call" | custom-call | flops 15000000512 | bytes 10000000 | tf_op jit(solution)/shard_map/forward/pallas_call | solution.py:154
  45.7 19.0 %middle.1 = (bf16[1024,512]{1,0:T(8,128)(2,1)}, f32[1024,512]{1,0:T(8,128)}, bf16[4,1024,128]{2,1,0:T(8,128)(2,1)}, f32[8,1024]{1,0:T(8,128)}, f32[1024,512]{1,0...) custom-call(f32[4,1024,128]{2,1,0:T(8,128)} %get-tuple-element.34.att_ref, ...), custom_call_target="tpu_custom_call" | custom-call | flops 15000000512 | bytes 20000000 | tf_op jit(solution)/shard_map/middle/pallas_call | solution.py:247
  66.4 18.6 %backward.1 = (bf16[4,1024,128]{2,1,0:T(8,128)(2,1)}, bf16[4,1024,128]{2,1,0:T(8,128)(2,1)}, bf16[4,1024,128]{2,1,0:T(8,128)(2,1)}) custom-call(s32[8]{0:T(128)} %fusion.ends_ref, bf16[4,1024,128]{2,1,0:T(8,128)(2,1)} %get-tuple-element.36.q_ref, bf16[4,1024,128]{2,1,0:T(8,128)(2,1)} %get-tuple-element.37.k_ref, ...), custom_call_target="tpu_custom_call" | custom-call | flops 24000000000 | bytes 12000000 | tf_op jit(solution)/shard_map/backward/pallas_call | solution.py:311
  85.0 8.8 %last.1 = (bf16[1024,512]{1,0:T(8,128)(2,1)}, f32[512,1536]{1,0:T(8,128)}, f32[8,512]{1,0:T(8,128)}) custom-call(bf16[4,1024,128]{2,1,0:T(8,128)(2,1)} %get-tuple-element.42.dq_ref, bf16[4,1024,128]{2,1,0:T(8,128)(2,1)} %get-tuple-element.43.dk_ref, bf16[4,1024,128]{2,1,0:T(8,128)(2,1)} %get-tuple-element.44.dv_ref, ...), custom_call_target="tpu_custom_call" | custom-call | flops 8000000000 | bytes 12000000 | tf_op jit(solution)/shard_map/last/pallas_call | solution.py:353
  94.6 2.2 fusion.3
  99.6 1.8 collective-permute-start.1
  101.4 1.9 collective-permute-start.2
  105.3 4.3 %all-to-all-start.3 = ((bf16[4,256,512]{2,1,0:T(8,128)(2,1)}), bf16[4,256,512]{2,1,0:T(8,128)(2,1)}, u32[]{:S(2)}, u32[]{:S(2)}) async-start(bf16[4,256,512]{2,1,0:T(8,128)(2,1)} %bitcast.90), calls=%async_computation.3 | async-start | bytes 2097152 | tf_op jit(solution)/shard_map/all_to_all | solution.py:442
  111.2 2.3 %collective-permute-start.5 = (f32[16,512]{1,0:T(8,128)S(1)}, f32[16,512]{1,0:T(8,128)S(1)}, u32[]{:S(2)}, u32[]{:S(2)}) collective-permute-start(f32[16,512]{1,0:T(8,128)S(1)} %add_add_fusion.1), channel_id=1, source_target_pairs={{0,16},{1,17},{2,18},{3,19},{4,20},{5,21},{6,22},{7,23},{8,24},{9,... | collective-permute-start | bytes 98312 | tf_op jit(solution)/shard_map/ppermute | solution.py:380
  116.2 2.4 %collective-permute-start.10 = (bf16[192,512]{1,0:T(8,128)(2,1)S(1)}, bf16[192,512]{1,0:T(8,128)(2,1)S(1)}, u32[]{:S(2)}, u32[]{:S(2)}) collective-permute-start(bf16[192,512]{1,0:T(8,128)(2,1)S(1)} %get-tuple-element.73), channel_id=1, source_target_pairs={{0,6},{1,7},{2,4},{3,5},{4,2},{5,3},{6,0},{7,1},{8,14},{9,15},{10,... | collective-permute-start | bytes 589832 | tf_op jit(solution)/shard_map/ppermute | solution.py:380
  119.0 8.4 %all-to-all-done.3 = bf16[4,256,512]{2,1,0:T(8,128)(2,1)} async-done(((bf16[4,256,512]{2,1,0:T(8,128)(2,1)}), bf16[4,256,512]{2,1,0:T(8,128)(2,1)}, u32[]{:S(2)}, u32[]{:S(2)}) %all-to-all-start.3) | async-done | bytes 1048608 | tf_op jit(solution)/shard_map/all_to_all | solution.py:442
  127.4 4.8 %all-to-all-start.2 = ((bf16[4,256,512]{2,1,0:T(8,128)(2,1)}), bf16[4,256,512]{2,1,0:T(8,128)(2,1)S(1)}, u32[]{:S(2)}, u32[]{:S(2)}) async-start(bf16[4,256,512]{2,1,0:T(8,128)(2,1)} %bitcast.89), calls=%async_computation.2 | async-start | bytes 2097152 | tf_op jit(solution)/shard_map/all_to_all | solution.py:442
  135.0 2.3 %collective-permute-start.12 = (bf16[48,512]{1,0:T(8,128)(2,1)S(1)}, bf16[48,512]{1,0:T(8,128)(2,1)S(1)}, u32[]{:S(2)}, u32[]{:S(2)}) collective-permute-start(bf16[48,512]{1,0:T(8,128)(2,1)S(1)} %get-tuple-element.80), channel_id=1, source_target_pairs={{0,16},{1,17},{2,18},{3,19},{4,20},{5,21},{6,22},{7,23},{8,24},{9,... | collective-permute-start | bytes 147464 | tf_op jit(solution)/shard_map/ppermute | solution.py:380
  139.1 3.1 %collective-permute-done.13 = bf16[48,512]{1,0:T(8,128)(2,1)S(1)} collective-permute-done((bf16[48,512]{1,0:T(8,128)(2,1)S(1)}, bf16[48,512]{1,0:T(8,128)(2,1)S(1)}, u32[]{:S(2)}, u32[]{:S(2)}) %collective-permute-start.13) | collective-permute-done | bytes 49184 | tf_op jit(solution)/shard_map/ppermute | solution.py:380
  142.9 2.8 %convert_element_type.105 = f32[4,256,512]{2,1,0:T(8,128)} convert(bf16[4,256,512]{2,1,0:T(8,128)(2,1)} %all-to-all-done.3) | non-fusion elementwise | flops 524288 | bytes 3145728 | tf_op jit(solution)/shard_map/convert_element_type | solution.py:453
  145.8 2.6 %collective-permute-start.15 = (bf16[48,512]{1,0:T(8,128)(2,1)S(1)}, bf16[48,512]{1,0:T(8,128)(2,1)S(1)}, u32[]{:S(2)}, u32[]{:S(2)}) collective-permute-start(bf16[48,512]{1,0:T(8,128)(2,1)S(1)} %get-tuple-element.57), channel_id=1, source_target_pairs={{0,16},{1,17},{2,18},{3,19},{4,20},{5,21},{6,22},{7,23},{8,24},{9,... | collective-permute-start | bytes 147464 | tf_op jit(solution)/shard_map/ppermute | solution.py:380
  149.9 3.7 %collective-permute-done.16 = bf16[48,512]{1,0:T(8,128)(2,1)S(1)} collective-permute-done((bf16[48,512]{1,0:T(8,128)(2,1)S(1)}, bf16[48,512]{1,0:T(8,128)(2,1)S(1)}, u32[]{:S(2)}, u32[]{:S(2)}) %collective-permute-start.16) | collective-permute-done | bytes 49184 | tf_op jit(solution)/shard_map/ppermute | solution.py:380
  156.4 2.6 %convert_add_fusion = f32[1280,512]{1,0:T(8,128)S(1)} fusion(bf16[1280,512]{1,0:T(8,128)(2,1)} %collective-permute-done.21, f32[2560,512]{1,0:T(8,128)} %copy-done, s32[]{:T(128)S(6)} %select_n.125), kind=kLoop, calls=%fused_computation.4 | loop fusion | flops 1310720 | bytes 6553604 | tf_op jit(solution)/shard_map/add | solution.py:393
  161.9 8.2 %collective-permute-done.22 = bf16[320,512]{1,0:T(8,128)(2,1)S(1)} collective-permute-done((bf16[320,512]{1,0:T(8,128)(2,1)S(1)}, bf16[320,512]{1,0:T(8,128)(2,1)S(1)}, u32[]{:S(2)}, u32[]{:S(2)}) %collective-permute-start.22) | collective-permute-done | bytes 327712 | tf_op jit(solution)/shard_map/ppermute | solution.py:380
  170.1 7.2 %collective-permute-done.24 = bf16[320,512]{1,0:T(8,128)(2,1)S(1)} collective-permute-done((bf16[320,512]{1,0:T(8,128)(2,1)S(1)}, bf16[320,512]{1,0:T(8,128)(2,1)S(1)}, u32[]{:S(2)}, u32[]{:S(2)}) %collective-permute-start.24) | collective-permute-done | bytes 327712 | tf_op jit(solution)/shard_map/ppermute | solution.py:380
  177.6 1.8 collective-permute-start.26
  179.4 1.8 collective-permute-start.27
  181.2 4.0 %collective-permute-start.20 = (bf16[768,512]{1,0:T(8,128)(2,1)S(1)}, bf16[768,512]{1,0:T(8,128)(2,1)S(1)}, u32[]{:S(2)}, u32[]{:S(2)}) collective-permute-start(bf16[768,512]{1,0:T(8,128)(2,1)S(1)} %bitcast.80), channel_id=1, source_target_pairs={{0,1},{1,0},{2,3},{3,2},{4,5},{5,4},{6,7},{7,6},{8,9},{9,8},{10,11... | collective-permute-start | bytes 2359304 | tf_op jit(solution)/shard_map/ppermute | solution.py:380
  185.9 1.8 collective-permute-start.29
  190.1 2.8 %collective-permute-done.30 = bf16[80,512]{1,0:T(8,128)(2,1)S(1)} collective-permute-done((bf16[80,512]{1,0:T(8,128)(2,1)S(1)}, bf16[80,512]{1,0:T(8,128)(2,1)S(1)}, u32[]{:S(2)}, u32[]{:S(2)}) %collective-permute-start.30) | collective-permute-done | bytes 81952 | tf_op jit(solution)/shard_map/ppermute | solution.py:380
  195.9 3.1 %collective-permute-done.31 = bf16[320,512]{1,0:T(8,128)(2,1)S(1)} collective-permute-done((bf16[320,512]{1,0:T(8,128)(2,1)S(1)}, bf16[320,512]{1,0:T(8,128)(2,1)S(1)}, u32[]{:S(2)}, u32[]{:S(2)}) %collective-permute-start.31) | collective-permute-done | bytes 327712 | tf_op jit(solution)/shard_map/ppermute | solution.py:380
  199.1 4.7 %collective-permute-done.33 = bf16[320,512]{1,0:T(8,128)(2,1)S(1)} collective-permute-done((bf16[320,512]{1,0:T(8,128)(2,1)S(1)}, bf16[320,512]{1,0:T(8,128)(2,1)S(1)}, u32[]{:S(2)}, u32[]{:S(2)}) %collective-permute-start.33) | collective-permute-done | bytes 327712 | tf_op jit(solution)/shard_map/ppermute | solution.py:380
  203.8 7.6 %collective-permute-start.34 = (bf16[1280,512]{1,0:T(8,128)(2,1)S(1)}, bf16[1280,512]{1,0:T(8,128)(2,1)S(1)}, u32[]{:S(2)}, u32[]{:S(2)}) collective-permute-start(bf16[1280,512]{1,0:T(8,128)(2,1)S(1)} %bitcast.78), channel_id=1, source_target_pairs={{0,1},{1,0},{2,3},{3,2},{4,5},{5,4},{6,7},{7,6},{8,9},{9,8},{10,11... | collective-permute-start | bytes 3932168 | tf_op jit(solution)/shard_map/ppermute | solution.py:380
  212.3 1.9 pad_maximum_fusion.2
  (124 shorter events, 40.0 us)
Async XLA Ops:
  0.7 17.7 %all-to-all-start = ((bf16[4,256,512]{2,1,0:T(8,128)(2,1)}), bf16[4,256,512]{2,1,0:T(8,128)(2,1)S(1)}, u32[]{:S(2)}, u32[]{:S(2)}) async-start(bf16[4,256,512]{2,1,0:T(8,128)(2,1)} %param.15), calls=%async_computation | async-start | bytes 2097152 | tf_op jit(solution)/shard_map/all_to_all | solution.py:442
  18.3 26.4 %all-to-all-start.1 = ((bf16[4,256,512]{2,1,0:T(8,128)(2,1)}), bf16[4,256,512]{2,1,0:T(8,128)(2,1)S(1)}, u32[]{:S(2)}, u32[]{:S(2)}) async-start(bf16[4,256,512]{2,1,0:T(8,128)(2,1)} %param.29), calls=%async_computation.1 | async-start | bytes 2097152 | tf_op jit(solution)/shard_map/all_to_all | solution.py:442
  98.1 15.5 %collective-permute-start.7 = (bf16[768,512]{1,0:T(8,128)(2,1)}, bf16[768,512]{1,0:T(8,128)(2,1)}, u32[]{:S(2)}, u32[]{:S(2)}) collective-permute-start(bf16[768,512]{1,0:T(8,128)(2,1)} %dynamic-slice_convert_fusion.1), channel_id=1, source_target_pairs={{0,1},{1,0},{2,3},{3,2},{4,5},{5,4},{6,7},{7,6},{8,9},{9,8},{10,11... | collective-permute-start | bytes 2359304 | tf_op jit(solution)/shard_map/ppermute | solution.py:380
  99.6 9.9 %collective-permute-start.1 = (f32[16,512]{1,0:T(8,128)S(1)}, f32[16,512]{1,0:T(8,128)S(1)}, u32[]{:S(2)}, u32[]{:S(2)}) collective-permute-start(f32[16,512]{1,0:T(8,128)S(1)} %add.172), channel_id=1, source_target_pairs={{0,2},{1,3},{2,0},{3,1},{4,6},{5,7},{6,4},{7,5},{8,10},{9,11},{10,... | collective-permute-start | bytes 98312 | tf_op jit(solution)/shard_map/ppermute | solution.py:380
  101.4 8.1 %collective-permute-start.2 = (f32[16,512]{1,0:T(8,128)S(1)}, f32[16,512]{1,0:T(8,128)S(1)}, u32[]{:S(2)}, u32[]{:S(2)}) collective-permute-start(f32[16,512]{1,0:T(8,128)S(1)} %add.172), channel_id=1, source_target_pairs={{0,4},{1,5},{2,6},{3,7},{4,0},{5,1},{6,2},{7,3},{8,12},{9,13},{10,... | collective-permute-start | bytes 98312 | tf_op jit(solution)/shard_map/ppermute | solution.py:380
  103.3 6.2 %collective-permute-start.3 = (f32[16,512]{1,0:T(8,128)S(1)}, f32[16,512]{1,0:T(8,128)S(1)}, u32[]{:S(2)}, u32[]{:S(2)}) collective-permute-start(f32[16,512]{1,0:T(8,128)S(1)} %add.172), channel_id=1, source_target_pairs={{0,6},{1,7},{2,4},{3,5},{4,2},{5,3},{6,0},{7,1},{8,14},{9,15},{10,... | collective-permute-start | bytes 98312 | tf_op jit(solution)/shard_map/ppermute | solution.py:380
  104.5 51.8 %collective-permute-start.21 = (bf16[1280,512]{1,0:T(8,128)(2,1)}, bf16[1280,512]{1,0:T(8,128)(2,1)}, u32[]{:S(2)}, u32[]{:S(2)}) collective-permute-start(bf16[1280,512]{1,0:T(8,128)(2,1)} %dynamic-slice_convert_fusion), channel_id=1, source_target_pairs={{0,1},{1,0},{2,3},{3,2},{4,5},{5,4},{6,7},{7,6},{8,9},{9,8},{10,11... | collective-permute-start | bytes 3932168 | tf_op jit(solution)/shard_map/ppermute | solution.py:380
  105.3 22.1 %all-to-all-start.3 = ((bf16[4,256,512]{2,1,0:T(8,128)(2,1)}), bf16[4,256,512]{2,1,0:T(8,128)(2,1)}, u32[]{:S(2)}, u32[]{:S(2)}) async-start(bf16[4,256,512]{2,1,0:T(8,128)(2,1)} %bitcast.90), calls=%async_computation.3 | async-start | bytes 2097152 | tf_op jit(solution)/shard_map/all_to_all | solution.py:442
  109.6 9.0 %collective-permute-start.4 = (f32[16,512]{1,0:T(8,128)S(1)}, f32[16,512]{1,0:T(8,128)S(1)}, u32[]{:S(2)}, u32[]{:S(2)}) collective-permute-start(f32[16,512]{1,0:T(8,128)S(1)} %add_add_fusion.1), channel_id=1, source_target_pairs={{0,8},{1,9},{2,10},{3,11},{4,12},{5,13},{6,14},{7,15},{8,0},{9,1},... | collective-permute-start | bytes 98312 | tf_op jit(solution)/shard_map/ppermute | solution.py:380
  111.2 7.4 %collective-permute-start.5 = (f32[16,512]{1,0:T(8,128)S(1)}, f32[16,512]{1,0:T(8,128)S(1)}, u32[]{:S(2)}, u32[]{:S(2)}) collective-permute-start(f32[16,512]{1,0:T(8,128)S(1)} %add_add_fusion.1), channel_id=1, source_target_pairs={{0,16},{1,17},{2,18},{3,19},{4,20},{5,21},{6,22},{7,23},{8,24},{9,... | collective-permute-start | bytes 98312 | tf_op jit(solution)/shard_map/ppermute | solution.py:380
  113.6 5.4 %collective-permute-start.6 = (f32[16,512]{1,0:T(8,128)S(1)}, f32[16,512]{1,0:T(8,128)S(1)}, u32[]{:S(2)}, u32[]{:S(2)}) collective-permute-start(f32[16,512]{1,0:T(8,128)S(1)} %add_add_fusion.1), channel_id=1, source_target_pairs={{0,24},{1,25},{2,26},{3,27},{4,28},{5,29},{6,30},{7,31},{8,16},{9,... | collective-permute-start | bytes 98312 | tf_op jit(solution)/shard_map/ppermute | solution.py:380
  116.2 16.0 %collective-permute-start.10 = (bf16[192,512]{1,0:T(8,128)(2,1)S(1)}, bf16[192,512]{1,0:T(8,128)(2,1)S(1)}, u32[]{:S(2)}, u32[]{:S(2)}) collective-permute-start(bf16[192,512]{1,0:T(8,128)(2,1)S(1)} %get-tuple-element.73), channel_id=1, source_target_pairs={{0,6},{1,7},{2,4},{3,5},{4,2},{5,3},{6,0},{7,1},{8,14},{9,15},{10,... | collective-permute-start | bytes 589832 | tf_op jit(solution)/shard_map/ppermute | solution.py:380
  118.6 13.7 %collective-permute-start.8 = (bf16[192,512]{1,0:T(8,128)(2,1)S(1)}, bf16[192,512]{1,0:T(8,128)(2,1)S(1)}, u32[]{:S(2)}, u32[]{:S(2)}) collective-permute-start(bf16[192,512]{1,0:T(8,128)(2,1)S(1)} %get-tuple-element.72), channel_id=1, source_target_pairs={{0,2},{1,3},{2,0},{3,1},{4,6},{5,7},{6,4},{7,5},{8,10},{9,11},{10,... | collective-permute-start | bytes 589832 | tf_op jit(solution)/shard_map/ppermute | solution.py:380
  118.6 13.6 %collective-permute-start.9 = (bf16[192,512]{1,0:T(8,128)(2,1)S(1)}, bf16[192,512]{1,0:T(8,128)(2,1)S(1)}, u32[]{:S(2)}, u32[]{:S(2)}) collective-permute-start(bf16[192,512]{1,0:T(8,128)(2,1)S(1)} %get-tuple-element.74), channel_id=1, source_target_pairs={{0,4},{1,5},{2,6},{3,7},{4,0},{5,1},{6,2},{7,3},{8,12},{9,13},{10,... | collective-permute-start | bytes 589832 | tf_op jit(solution)/shard_map/ppermute | solution.py:380
  127.4 18.4 %all-to-all-start.2 = ((bf16[4,256,512]{2,1,0:T(8,128)(2,1)}), bf16[4,256,512]{2,1,0:T(8,128)(2,1)S(1)}, u32[]{:S(2)}, u32[]{:S(2)}) async-start(bf16[4,256,512]{2,1,0:T(8,128)(2,1)} %bitcast.89), calls=%async_computation.2 | async-start | bytes 2097152 | tf_op jit(solution)/shard_map/all_to_all | solution.py:442
  142.2 7.3 %collective-permute-start.14 = (bf16[48,512]{1,0:T(8,128)(2,1)S(1)}, bf16[48,512]{1,0:T(8,128)(2,1)S(1)}, u32[]{:S(2)}, u32[]{:S(2)}) collective-permute-start(bf16[48,512]{1,0:T(8,128)(2,1)S(1)} %get-tuple-element.57), channel_id=1, source_target_pairs={{0,8},{1,9},{2,10},{3,11},{4,12},{5,13},{6,14},{7,15},{8,0},{9,1},... | collective-permute-start | bytes 147464 | tf_op jit(solution)/shard_map/ppermute | solution.py:380
  148.4 5.2 %collective-permute-start.16 = (bf16[48,512]{1,0:T(8,128)(2,1)S(1)}, bf16[48,512]{1,0:T(8,128)(2,1)S(1)}, u32[]{:S(2)}, u32[]{:S(2)}) collective-permute-start(bf16[48,512]{1,0:T(8,128)(2,1)S(1)} %get-tuple-element.57), channel_id=1, source_target_pairs={{0,24},{1,25},{2,26},{3,27},{4,28},{5,29},{6,30},{7,31},{8,16},{9,... | collective-permute-start | bytes 147464 | tf_op jit(solution)/shard_map/ppermute | solution.py:380
  153.6 6.8 %collective-permute-start.17 = (bf16[192,512]{1,0:T(8,128)(2,1)S(1)}, bf16[192,512]{1,0:T(8,128)(2,1)S(1)}, u32[]{:S(2)}, u32[]{:S(2)}) collective-permute-start(bf16[192,512]{1,0:T(8,128)(2,1)S(1)} %bitcast.92), channel_id=1, source_target_pairs={{0,2},{1,3},{2,0},{3,1},{4,6},{5,7},{6,4},{7,5},{8,10},{9,11},{10,... | collective-permute-start | bytes 589832 | tf_op jit(solution)/shard_map/ppermute | solution.py:380
  153.6 8.2 %collective-permute-start.18 = (bf16[192,512]{1,0:T(8,128)(2,1)S(1)}, bf16[192,512]{1,0:T(8,128)(2,1)S(1)}, u32[]{:S(2)}, u32[]{:S(2)}) collective-permute-start(bf16[192,512]{1,0:T(8,128)(2,1)S(1)} %bitcast.93), channel_id=1, source_target_pairs={{0,4},{1,5},{2,6},{3,7},{4,0},{5,1},{6,2},{7,3},{8,12},{9,13},{10,... | collective-permute-start | bytes 589832 | tf_op jit(solution)/shard_map/ppermute | solution.py:380
  154.9 26.3 %collective-permute-start.19 = (bf16[192,512]{1,0:T(8,128)(2,1)S(1)}, bf16[192,512]{1,0:T(8,128)(2,1)S(1)}, u32[]{:S(2)}, u32[]{:S(2)}) collective-permute-start(bf16[192,512]{1,0:T(8,128)(2,1)S(1)} %bitcast.94), channel_id=1, source_target_pairs={{0,6},{1,7},{2,4},{3,5},{4,2},{5,3},{6,0},{7,1},{8,14},{9,15},{10,... | collective-permute-start | bytes 589832 | tf_op jit(solution)/shard_map/ppermute | solution.py:380
  159.1 11.0 %collective-permute-start.22 = (bf16[320,512]{1,0:T(8,128)(2,1)S(1)}, bf16[320,512]{1,0:T(8,128)(2,1)S(1)}, u32[]{:S(2)}, u32[]{:S(2)}) collective-permute-start(bf16[320,512]{1,0:T(8,128)(2,1)S(1)} %get-tuple-element.67), channel_id=1, source_target_pairs={{0,2},{1,3},{2,0},{3,1},{4,6},{5,7},{6,4},{7,5},{8,10},{9,11},{10,... | collective-permute-start | bytes 983048 | tf_op jit(solution)/shard_map/ppermute | solution.py:380
  159.2 10.9 %collective-permute-start.23 = (bf16[320,512]{1,0:T(8,128)(2,1)S(1)}, bf16[320,512]{1,0:T(8,128)(2,1)S(1)}, u32[]{:S(2)}, u32[]{:S(2)}) collective-permute-start(bf16[320,512]{1,0:T(8,128)(2,1)S(1)} %get-tuple-element.69), channel_id=1, source_target_pairs={{0,4},{1,5},{2,6},{3,7},{4,0},{5,1},{6,2},{7,3},{8,12},{9,13},{10,... | collective-permute-start | bytes 983048 | tf_op jit(solution)/shard_map/ppermute | solution.py:380
  160.4 16.8 %collective-permute-start.24 = (bf16[320,512]{1,0:T(8,128)(2,1)S(1)}, bf16[320,512]{1,0:T(8,128)(2,1)S(1)}, u32[]{:S(2)}, u32[]{:S(2)}) collective-permute-start(bf16[320,512]{1,0:T(8,128)(2,1)S(1)} %get-tuple-element.68), channel_id=1, source_target_pairs={{0,6},{1,7},{2,4},{3,5},{4,2},{5,3},{6,0},{7,1},{8,14},{9,15},{10,... | collective-permute-start | bytes 983048 | tf_op jit(solution)/shard_map/ppermute | solution.py:380
  177.5 7.6 %collective-permute-start.25 = (bf16[80,512]{1,0:T(8,128)(2,1)S(1)}, bf16[80,512]{1,0:T(8,128)(2,1)S(1)}, u32[]{:S(2)}, u32[]{:S(2)}) collective-permute-start(bf16[80,512]{1,0:T(8,128)(2,1)S(1)} %get-tuple-element.75), channel_id=1, source_target_pairs={{0,8},{1,9},{2,10},{3,11},{4,12},{5,13},{6,14},{7,15},{8,0},{9,1},... | collective-permute-start | bytes 245768 | tf_op jit(solution)/shard_map/ppermute | solution.py:380
  177.6 7.6 %collective-permute-start.26 = (bf16[80,512]{1,0:T(8,128)(2,1)S(1)}, bf16[80,512]{1,0:T(8,128)(2,1)S(1)}, u32[]{:S(2)}, u32[]{:S(2)}) collective-permute-start(bf16[80,512]{1,0:T(8,128)(2,1)S(1)} %get-tuple-element.77), channel_id=1, source_target_pairs={{0,16},{1,17},{2,18},{3,19},{4,20},{5,21},{6,22},{7,23},{8,24},{9,... | collective-permute-start | bytes 245768 | tf_op jit(solution)/shard_map/ppermute | solution.py:380
  179.4 5.8 %collective-permute-start.27 = (bf16[80,512]{1,0:T(8,128)(2,1)S(1)}, bf16[80,512]{1,0:T(8,128)(2,1)S(1)}, u32[]{:S(2)}, u32[]{:S(2)}) collective-permute-start(bf16[80,512]{1,0:T(8,128)(2,1)S(1)} %get-tuple-element.76), channel_id=1, source_target_pairs={{0,24},{1,25},{2,26},{3,27},{4,28},{5,29},{6,30},{7,31},{8,16},{9,... | collective-permute-start | bytes 245768 | tf_op jit(solution)/shard_map/ppermute | solution.py:380
  181.2 14.6 %collective-permute-start.20 = (bf16[768,512]{1,0:T(8,128)(2,1)S(1)}, bf16[768,512]{1,0:T(8,128)(2,1)S(1)}, u32[]{:S(2)}, u32[]{:S(2)}) collective-permute-start(bf16[768,512]{1,0:T(8,128)(2,1)S(1)} %bitcast.80), channel_id=1, source_target_pairs={{0,1},{1,0},{2,3},{3,2},{4,5},{5,4},{6,7},{7,6},{8,9},{9,8},{10,11... | collective-permute-start | bytes 2359304 | tf_op jit(solution)/shard_map/ppermute | solution.py:380
  187.6 5.3 %collective-permute-start.30 = (bf16[80,512]{1,0:T(8,128)(2,1)S(1)}, bf16[80,512]{1,0:T(8,128)(2,1)S(1)}, u32[]{:S(2)}, u32[]{:S(2)}) collective-permute-start(bf16[80,512]{1,0:T(8,128)(2,1)S(1)} %get-tuple-element.55), channel_id=1, source_target_pairs={{0,24},{1,25},{2,26},{3,27},{4,28},{5,29},{6,30},{7,31},{8,16},{9,... | collective-permute-start | bytes 245768 | tf_op jit(solution)/shard_map/ppermute | solution.py:380
  192.9 6.0 %collective-permute-start.31 = (bf16[320,512]{1,0:T(8,128)(2,1)S(1)}, bf16[320,512]{1,0:T(8,128)(2,1)S(1)}, u32[]{:S(2)}, u32[]{:S(2)}) collective-permute-start(bf16[320,512]{1,0:T(8,128)(2,1)S(1)} %bitcast.82), channel_id=1, source_target_pairs={{0,2},{1,3},{2,0},{3,1},{4,6},{5,7},{6,4},{7,5},{8,10},{9,11},{10,... | collective-permute-start | bytes 983048 | tf_op jit(solution)/shard_map/ppermute | solution.py:380
  193.1 5.9 %collective-permute-start.32 = (bf16[320,512]{1,0:T(8,128)(2,1)S(1)}, bf16[320,512]{1,0:T(8,128)(2,1)S(1)}, u32[]{:S(2)}, u32[]{:S(2)}) collective-permute-start(bf16[320,512]{1,0:T(8,128)(2,1)S(1)} %bitcast.83), channel_id=1, source_target_pairs={{0,4},{1,5},{2,6},{3,7},{4,0},{5,1},{6,2},{7,3},{8,12},{9,13},{10,... | collective-permute-start | bytes 983048 | tf_op jit(solution)/shard_map/ppermute | solution.py:380
  194.4 9.4 %collective-permute-start.33 = (bf16[320,512]{1,0:T(8,128)(2,1)S(1)}, bf16[320,512]{1,0:T(8,128)(2,1)S(1)}, u32[]{:S(2)}, u32[]{:S(2)}) collective-permute-start(bf16[320,512]{1,0:T(8,128)(2,1)S(1)} %bitcast.84), channel_id=1, source_target_pairs={{0,6},{1,7},{2,4},{3,5},{4,2},{5,3},{6,0},{7,1},{8,14},{9,15},{10,... | collective-permute-start | bytes 983048 | tf_op jit(solution)/shard_map/ppermute | solution.py:380
  203.8 10.7 %collective-permute-start.34 = (bf16[1280,512]{1,0:T(8,128)(2,1)S(1)}, bf16[1280,512]{1,0:T(8,128)(2,1)S(1)}, u32[]{:S(2)}, u32[]{:S(2)}) collective-permute-start(bf16[1280,512]{1,0:T(8,128)(2,1)S(1)} %bitcast.78), channel_id=1, source_target_pairs={{0,1},{1,0},{2,3},{3,2},{4,5},{5,4},{6,7},{7,6},{8,9},{9,8},{10,11... | collective-permute-start | bytes 3932168 | tf_op jit(solution)/shard_map/ppermute | solution.py:380
  (15 other events, 51.0 us)
